TPU v7x, 32 devices: a whole 2x2x4 slice. The times are simulated.
32 devices in a mesh: ctx: 16 (over z, y, x), ch: 2 (over core).
Axes of the slice: x: 2, y: 2, z: 4, core: 2. Of those that a mesh axis runs over, the one named last changes fastest.
Arguments:
- query: bfloat16 [2048, 4096], P('ctx', 'ch'), may hold values from -6 to 6
- key: bfloat16 [2048, 4096], P('ctx', 'ch'), may hold values from -6 to 6
- value: bfloat16 [2048, 4096], P('ctx', 'ch'), may hold values from -6 to 6
- filter_taps: float32 [2048, 256], P('ctx', 'ch'), may hold values from -0.125 to 0.125
- conv_bias: float32 [4096], P('ch'), may hold values from -4 to 4
- norm_gain: float32 [4096], P('ch'), may hold values from 0.1 to 1.9
- pair_list: int32 [136, 3], replicated, may hold values from 0 to 15, as said below
Outputs:
- mixed: bfloat16 [2048, 4096], P('ctx', 'ch')
Inputs may be any that keep to these rules, and one draw needn't show every extreme that they name: `pair_list`: every pair of blocks with source <= target appears once, in no particular order. A row with source = target names the device that holds that block; blocks c and 15 - c are held by two devices whose indices differ only in the lowest bit. Every other pair is executed by one of those two devices for its target block. Each device executes at most 9 pairs.
All inputs are finite; a program needn't handle non-finite values.
Results may differ from a plain program's by a relative error of at most 0.0049.
Values may be sent and summed in bfloat16 or wider, within the bound.
A program may use at most 64 MiB of HBM per device.

v0:
```python
import functools

import jax
import jax.numpy as jnp
from jax import lax
from jax.experimental import pallas as pl
from jax.experimental.pallas import tpu as pltpu
from jax.sharding import PartitionSpec as P

MESH = pl.DeviceIdType.MESH
LANES = 128
VMEM_BYTES = 852 * 64 * 1024
STRIP = 8
F32 = jnp.float32
BF16 = jnp.bfloat16


class Plan:
    def __init__(self, mesh, channels, filters, rows):
        self.blocks = mesh.shape["ctx"]
        self.halves = mesh.shape["ch"]
        self.rows = rows
        self.channels = channels
        self.filters = filters
        self.group = channels // filters
        self.each = max(1, filters // self.blocks)
        self.workers = filters // self.each
        self.share = self.each * self.group
        self.parts = 4 if self.each % 4 == 0 else 1
        self.each_part = self.each // self.parts
        self.share_part = self.share // self.parts
        self.span = channels // self.parts


def kernel(plan, pairs, query, key, value, taps, bias, gain, out, *scratch):
    blocks, rows, group, span = plan.blocks, plan.rows, plan.group, plan.span
    part_rows = plan.share_part
    parts = range(plan.parts)
    scratch = list(scratch)
    take = lambda count: [scratch.pop(0) for _ in range(count)]
    pairs_here, table, table_here, query_here, key_here, value_here, taps_here, bias_here = take(8)
    gain_here, gated = take(2)
    flipped, taps_rows, taps_flipped, taps_got, toeplitz, total, results, squares = take(8)
    got, ordered, made, staged = (take(plan.parts) for _ in range(4))
    taps_send, taps_recv, square_send, square_recv, loaded, loaded_part = take(6)
    go_send, go_recv, back_send, back_recv = take(4)

    me = lax.axis_index("ctx")
    half = lax.axis_index("ch")

    def only_worker(index):
        if plan.workers == blocks:
            return lambda fn: fn()
        return pl.when(index < plan.workers)

    def slot_of(step):
        return lax.rem(me + step, blocks)

    bits = [1 << place for place in range((blocks - 1).bit_length())]
    digits = [lax.rem(lax.div(me, bit), 2) for bit in bits]

    def peer_of(mask):
        peer = me
        for bit, digit in zip(bits, digits):
            flip = (mask // bit) % 2 if isinstance(mask, int) else lax.rem(lax.div(mask, bit), 2)
            peer = peer + flip * bit * (1 - 2 * digit)
        return peer

    near = [peer_of(blocks - step) for step in range(1, blocks)] if blocks <= 16 else None

    def each_peer(act):
        if near is not None:
            for peer in near:
                act(peer)
        else:
            pl.loop(1, blocks)(lambda step: act(peer_of(blocks - step)))

    def spread(count, act):
        if count <= 16:
            for index in range(count):
                act(index)
        else:
            pl.loop(0, count)(act)

    def column_copies(part):
        at = pl.ds(part * span, span)
        return [
            pltpu.make_async_copy(there.at[:, at], here.at[:, at], loaded_part.at[part, place])
            for place, (there, here) in enumerate(((key, key_here), (value, value_here)))
        ]

    whole_copies = [
        pltpu.make_async_copy(there, here, loaded.at[place])
        for place, (there, here) in enumerate(
            ((taps, taps_here), (pairs, pairs_here), (bias, bias_here), (query, query_here), (gain, gain_here))
        )
    ]
    taps_load, pairs_load, bias_load, query_load, gain_load = whole_copies
    table_load = pltpu.make_async_copy(table, table_here, loaded.at[5])

    strip = taps_flipped.shape[0] // plan.workers

    def strip_of(index):
        return pl.ds(pl.multiple_of(index * strip, strip), strip)

    def arrived(ref, sem):
        pltpu.make_async_remote_copy(
            src_ref=ref,
            dst_ref=ref,
            send_sem=sem,
            recv_sem=sem,
            device_id={"ctx": slot_of(1)},
            device_id_type=MESH,
        ).wait_recv()

    def from_others(wait):
        if plan.workers == blocks:
            wait(blocks - 1)
        else:
            pl.when(me < plan.workers)(lambda: wait(plan.workers - 1))
            pl.when(me >= plan.workers)(lambda: wait(plan.workers))

    def taps_copy(peer, slot):
        return pltpu.make_async_remote_copy(
            src_ref=taps_flipped.at[strip_of(peer)],
            dst_ref=taps_got.at[strip_of(slot)],
            send_sem=taps_send.at[0],
            recv_sem=taps_recv.at[0],
            device_id={"ctx": peer},
            device_id_type=MESH,
        )

    def go_copy(part, peer, slot):
        first = pl.multiple_of(part * span + peer * part_rows, group)
        return pltpu.make_async_remote_copy(
            src_ref=flipped.at[pl.ds(first, part_rows)],
            dst_ref=got[part].at[slot],
            send_sem=go_send.at[part],
            recv_sem=go_recv.at[part],
            device_id={"ctx": peer},
            device_id_type=MESH,
        )

    def back_copy(part, peer, slot):
        first = pl.multiple_of(part * span + slot * part_rows, group)
        return pltpu.make_async_remote_copy(
            src_ref=staged[part].at[peer],
            dst_ref=results.at[pl.ds(first, part_rows)],
            send_sem=back_send.at[part],
            recv_sem=back_recv.at[part],
            device_id={"ctx": peer},
            device_id_type=MESH,
        )

    def square_copy(peer, slot):
        return pltpu.make_async_remote_copy(
            src_ref=squares.at[half],
            dst_ref=squares.at[slot],
            send_sem=square_send.at[peer],
            recv_sem=square_recv.at[slot],
            device_id={"ch": peer},
            device_id_type=MESH,
        )

    barrier = pltpu.get_barrier_semaphore()

    @each_peer
    def _(peer):
        pl.semaphore_signal(barrier, inc=1, device_id={"ctx": peer}, device_id_type=MESH)

    for step in range(1, plan.halves):
        pl.semaphore_signal(
            barrier,
            inc=1,
            device_id={"ch": lax.rem(half + step, plan.halves)},
            device_id_type=MESH,
        )

    taps_load.start()
    for part in parts:
        for copy in column_copies(part):
            copy.start()
    for copy in (pairs_load, bias_load, query_load, gain_load):
        copy.start()

    taps_load.wait()
    taps_rows[...] = jnp.transpose(taps_here[...])

    for part in parts:
        for index in range(plan.each_part):
            row = part * (plan.filters // plan.parts) + index
            taps_flipped[pl.ds(part * plan.each_part + index, plan.workers, stride=strip), :] = (
                taps_rows[pl.ds(row, plan.workers, stride=plan.each_part), :]
            )

    def signal_tile(columns):
        return key_here[:, columns].astype(F32) * value_here[:, columns].astype(F32)

    part_tiles = span // LANES

    for part in parts:
        for copy in column_copies(part):
            copy.wait()

        for tile in range(part * part_tiles, (part + 1) * part_tiles):
            at = pl.ds(tile * LANES, LANES)
            flipped[at, :] = jnp.transpose(signal_tile(at)).astype(BF16)

        if part == 0:
            pl.semaphore_wait(barrier, blocks - 1 + plan.halves - 1)

            @each_peer
            def _(peer):
                @only_worker(peer)
                def _():
                    taps_copy(peer, me).start()

        @each_peer
        def _(peer, part=part):
            @only_worker(peer)
            def _():
                go_copy(part, peer, me).start()

    pairs_load.wait()
    source, target, runner = (pairs_here[place : place + 1, :] for place in range(3))
    slots = lax.broadcasted_iota(jnp.int32, (blocks, pairs_here.shape[1]), 0)
    diagonal = source == target
    device_of = jnp.where(diagonal & (source == slots), runner, 0)
    holder = jnp.where(diagonal & (runner == slots), source, 0)
    for place, found in enumerate((device_of, holder)):
        table[place * blocks : (place + 1) * blocks, :] = jnp.broadcast_to(
            jnp.sum(found, axis=1, keepdims=True), (blocks, LANES)
        )
    table_load.start()

    ahead = lax.broadcasted_iota(jnp.int32, (rows, LANES), 1) >= lax.broadcasted_iota(
        jnp.int32, (rows, LANES), 0
    )
    run = 8

    def spread_taps(part):
        @pl.loop(part * plan.each_part, (part + 1) * plan.each_part)
        def _(index):
            def some(step, before):
                for block in [step * run + place for place in range(run)]:
                    line = taps_got[pl.ds(block * strip + index, 1), :]
                    turned = pltpu.roll(
                        jnp.broadcast_to(line, (rows, LANES)), 0, 1, stride=1, stride_axis=0
                    )
                    at = pl.ds(pl.multiple_of(block * LANES, LANES), LANES)
                    toeplitz[index, :, at] = jnp.where(ahead, turned, before).astype(BF16)
                    before = turned
                return before

            lax.fori_loop(0, blocks // run, some, jnp.zeros((rows, LANES), F32))

    @only_worker(me)
    def _():
        taps_got[strip_of(me), :] = taps_flipped[strip_of(me), :]
        for part in parts:
            first = pl.multiple_of(part * span + me * part_rows, group)
            got[part][me] = flipped[pl.ds(first, part_rows), :]

        arrived(taps_got.at[pl.ds(0, (blocks - 1) * strip)], taps_recv.at[0])
        spread_taps(0)

    table_load.wait()

    @only_worker(me)
    def _():
        for part in parts:
            if part > 0:
                spread_taps(part)

            arrived(got[part].at[pl.ds(0, blocks - 1)], go_recv.at[part])

            def in_order(block, part=part):
                piece = got[part][table_here[block, 0]]
                at = pl.ds(block * group, group)
                for index in range(plan.each_part):
                    ordered[part][index, at, :] = piece[index * group : (index + 1) * group]

            spread(blocks, in_order)

            @pl.loop(0, plan.each_part)
            def _(index, part=part):
                for pair in range(blocks // 2):
                    height = (blocks - 2 * pair) * group
                    product = jnp.dot(
                        ordered[part][index, :height, :],
                        toeplitz[
                            part * plan.each_part + index,
                            :,
                            2 * pair * LANES : 2 * (pair + 1) * LANES,
                        ],
                        preferred_element_type=F32,
                    )
                    even, odd = 2 * pair * group, (2 * pair + 1) * group
                    if pair == 0:
                        total[...] = product[:, :LANES]
                    else:
                        total[even:, :] += product[:, :LANES]
                    total[odd:, :] += product[: height - group, LANES:]
                at = pl.ds(pl.multiple_of(index * group, group), group)
                made[part][:, at, :] = total[...].astype(BF16).reshape(blocks, group, LANES)

            @each_peer
            def _(peer, part=part):
                staged[part][peer] = made[part][table_here[blocks + peer, 0]]
                back_copy(part, peer, me).start()

            first = pl.multiple_of(part * span + me * part_rows, group)
            results[pl.ds(first, part_rows), :] = made[part][table_here[blocks + me, 0]]

    bias_load.wait()
    query_load.wait()
    sums = jnp.zeros((rows, LANES), F32)
    for part in parts:

        from_others(
            lambda count, part=part: arrived(
                results.at[pl.ds(part * span, count * part_rows)], back_recv.at[part]
            )
        )

        for tile in range(part * part_tiles, (part + 1) * part_tiles):
            at = pl.ds(tile * LANES, LANES)
            conv = jnp.transpose(results[at, :].astype(F32))
            signal = signal_tile(at).astype(BF16).astype(F32)
            product = query_here[:, at].astype(F32) * (conv + bias_here[:, at] * signal)
            gated[:, at] = product
            sums = sums + product * product

    squares[half] = jnp.broadcast_to(jnp.sum(sums, axis=1, keepdims=True), (rows, LANES))
    for step in range(1, plan.halves):
        square_copy(lax.rem(half + step, plan.halves), half).start()

    from_others(
        lambda count: arrived(taps_flipped.at[pl.ds(0, count * strip)], taps_send.at[0])
    )
    for part in parts:
        from_others(
            lambda count, part=part: arrived(
                flipped.at[pl.ds(part * span, count * part_rows)], go_send.at[part]
            )
        )

    @only_worker(me)
    def _():
        for part in parts:
            arrived(staged[part].at[pl.ds(0, blocks - 1)], back_send.at[part])

    for step in range(1, plan.halves):
        square_copy(half, lax.rem(half + step, plan.halves)).wait_recv()
    whole = squares[0]
    for other in range(1, plan.halves):
        whole = whole + squares[other]
    scaling = lax.rsqrt(whole / (plan.channels * plan.halves) + 1e-05)
    gain_load.wait()

    for tile in range(plan.channels // LANES):
        at = pl.ds(tile * LANES, LANES)
        out[:, at] = (gated[:, at] * scaling * gain_here[:, at]).astype(BF16)

    for step in range(1, plan.halves):
        square_copy(lax.rem(half + step, plan.halves), half).wait_send()


def body(mesh, query, key, value, filter_taps, conv_bias, norm_gain, pair_list):
    rows, channels = query.shape
    plan = Plan(mesh, channels, filter_taps.shape[1], rows)
    blocks, parts = plan.blocks, plan.parts
    vmem = pl.BlockSpec(memory_space=pltpu.VMEM)
    hbm = pl.BlockSpec(memory_space=pltpu.HBM)
    strip = max(STRIP, plan.each)
    part_piece = (blocks, plan.share_part, LANES)
    sems = pltpu.SemaphoreType.DMA
    scratch = [
        pltpu.VMEM(pair_list.shape[::-1], jnp.int32),
        pltpu.VMEM((2 * blocks, LANES), jnp.int32),
        pltpu.SMEM((2 * blocks, LANES), jnp.int32),
        pltpu.VMEM((rows, channels), BF16),
        pltpu.VMEM((rows, channels), BF16),
        pltpu.VMEM((rows, channels), BF16),
        pltpu.VMEM(filter_taps.shape, F32),
        pltpu.VMEM((1, channels), F32),
        pltpu.VMEM((1, channels), F32),
        pltpu.VMEM((rows, channels), F32),
        pltpu.VMEM((channels, LANES), BF16),
        pltpu.VMEM((plan.filters, LANES), F32),
        pltpu.VMEM((plan.workers * strip, LANES), F32),
        pltpu.VMEM((blocks * strip, LANES), F32),
        pltpu.VMEM((plan.each, rows, blocks * LANES), BF16),
        pltpu.VMEM((blocks * plan.group, LANES), F32),
        pltpu.VMEM((channels, LANES), BF16),
        pltpu.VMEM((plan.halves, rows, LANES), F32),
    ]
    scratch += [pltpu.VMEM(part_piece, BF16)] * parts
    scratch += [pltpu.VMEM((plan.each_part, blocks * plan.group, LANES), BF16)] * parts
    scratch += [pltpu.VMEM(part_piece, BF16)] * parts
    scratch += [pltpu.VMEM(part_piece, BF16)] * parts
    scratch += [sems((1,)), sems((1,)), sems((plan.halves,)), sems((plan.halves,))]
    scratch += [sems((6,)), sems((parts, 2))]
    scratch += [sems((parts,))] * 4
    pairs = blocks * (blocks + 2) // 4
    return pl.pallas_call(
        functools.partial(kernel, plan),
        out_shape=jax.ShapeDtypeStruct((rows, channels), BF16),
        in_specs=[hbm] * 7,
        out_specs=vmem,
        scratch_shapes=scratch,
        compiler_params=pltpu.CompilerParams(
            collective_id=0, has_side_effects=True, vmem_limit_bytes=VMEM_BYTES
        ),
        cost_estimate=pl.CostEstimate(
            flops=2 * plan.each * pairs * plan.group * rows * 2 * LANES,
            bytes_accessed=8 * rows * channels,
            transcendentals=0,
        ),
    )(pair_list.T, query, key, value, filter_taps, conv_bias[None, :], norm_gain[None, :])


def solution(mesh):
    placed = (P("ctx", "ch"), P("ctx", "ch"), P("ctx", "ch"), P("ctx", "ch"), P("ch"), P("ch"), P())
    return jax.shard_map(
        functools.partial(body, mesh),
        mesh=mesh,
        in_specs=placed,
        out_specs=P("ctx", "ch"),
        check_vma=False,
    )
```

profile of v0, /device:TPU:0, one launch (start us, length us, event | category | flops | bytes accessed | tf_op | source)
XLA Modules:
  0.0 36.9 jit_solution(708603190285634688)
XLA Ops:
  0.0 0.0 copy-start.3
  0.0 0.7 %copy-done.3 = s32[136,3]{0,1:T(4,128)S(1)} copy-done((s32[136,3]{0,1:T(4,128)S(1)}, s32[136,3]{0,1:T(4,128)}, u32[]{:S(2)}) %copy-start.3) | copy-done | bytes 1656
  0.7 0.0 copy-start
  0.7 0.8 %copy-done = f32[128,128]{1,0:T(8,128)S(1)} copy-done((f32[128,128]{1,0:T(8,128)S(1)}, f32[128,128]{1,0:T(8,128)}, u32[]{:S(2)}) %copy-start) | copy-done | bytes 65560
  1.5 0.0 copy-start.1
  1.5 0.7 %copy-done.1 = f32[2048]{0:T(1024)S(1)} copy-done((f32[2048]{0:T(1024)S(1)}, f32[2048]{0:T(1024)}, u32[]{:S(2)}) %copy-start.1) | copy-done | bytes 8216
  2.2 0.0 copy-start.2
  2.2 0.7 %copy-done.2 = f32[2048]{0:T(1024)S(1)} copy-done((f32[2048]{0:T(1024)S(1)}, f32[2048]{0:T(1024)}, u32[]{:S(2)}) %copy-start.2) | copy-done | bytes 8216
  2.9 33.2 %shard_map.73 = bf16[128,2048]{1,0:T(8,128)(2,1)S(1)} custom-call(s32[3,136]{1,0:T(4,128)S(1)} %bitcast.5, bf16[128,2048]{1,0:T(8,128)(2,1)} %query.1, bf16[128,2048]{1,0:T(8,128)(2,1)} %key.1, bf16[128,2048]{1,0:T(8,128)(2,1)} %value.1, f32[128,128]{1,0:T(8,128)S(1)} %copy-done, f32[1,2048]{1,0:T(1,128)S(1)} %bitcast.3, f32[1,2048]{1,0:T(1,128)S(1)} %bitcast.4), custom_call_target="tpu_custom_call" | custom-call | flops 603979776 | bytes 2097152 | tf_op jit(solution)/shard_map/pallas_call | solution.py:406
  36.1 0.8 %copy.9 = bf16[128,2048]{1,0:T(8,128)(2,1)} copy(bf16[128,2048]{1,0:T(8,128)(2,1)S(1)} %shard_map.73) | data formatting | bytes 1048576
Async XLA Ops:
  0.0 0.7 %copy-start.3 = (s32[136,3]{0,1:T(4,128)S(1)}, s32[136,3]{0,1:T(4,128)}, u32[]{:S(2)}) copy-start(s32[136,3]{0,1:T(4,128)} %param.13) | copy-start | bytes 4900
  0.7 0.8 %copy-start = (f32[128,128]{1,0:T(8,128)S(1)}, f32[128,128]{1,0:T(8,128)}, u32[]{:S(2)}) copy-start(f32[128,128]{1,0:T(8,128)} %taps.1) | copy-start | bytes 196612
  1.5 0.7 %copy-start.1 = (f32[2048]{0:T(1024)S(1)}, f32[2048]{0:T(1024)}, u32[]{:S(2)}) copy-start(f32[2048]{0:T(1024)} %param.11) | copy-start | bytes 24580
  2.2 0.7 %copy-start.2 = (f32[2048]{0:T(1024)S(1)}, f32[2048]{0:T(1024)}, u32[]{:S(2)}) copy-start(f32[2048]{0:T(1024)} %param.12) | copy-start | bytes 24580
where the time goes:
time: 37.3 us; the launch traced here: 36.9 us
  Pallas kernels  33.2 us (89%)
  local copies, waits for them, and re-layouts  3.71 us (10%)
    pallas_call x1, Pallas kernels, body(): pl.pallas_call(functools.partial(kernel, plan), out_shape=jax.ShapeDtypeS...  33.2 us
    unnamed x9, local copies, waits for them, and re-layouts  3.71 us

commit v1 on v0

--- a/solution.py
+++ b/solution.py
@@ -9,7 +9,7 @@
 
 MESH = pl.DeviceIdType.MESH
 LANES = 128
-VMEM_BYTES = 852 * 64 * 1024
+VMEM_BYTES = 1013 * 64 * 1024
 STRIP = 8
 F32 = jnp.float32
 BF16 = jnp.bfloat16
@@ -32,17 +32,17 @@
         self.span = channels // self.parts
 
 
-def kernel(plan, pairs, query, key, value, taps, bias, gain, out, *scratch):
+def kernel(plan, pairs, query, key, value, taps, bias, gated_out, scale, *scratch):
     blocks, rows, group, span = plan.blocks, plan.rows, plan.group, plan.span
     part_rows = plan.share_part
     parts = range(plan.parts)
     scratch = list(scratch)
     take = lambda count: [scratch.pop(0) for _ in range(count)]
     pairs_here, table, table_here, query_here, key_here, value_here, taps_here, bias_here = take(8)
-    gain_here, gated = take(2)
+    (gated,) = take(1)
     flipped, taps_rows, taps_flipped, taps_got, toeplitz, total, results, squares = take(8)
     got, ordered, made, staged = (take(plan.parts) for _ in range(4))
-    taps_send, taps_recv, square_send, square_recv, loaded, loaded_part = take(6)
+    taps_send, taps_recv, square_send, square_recv, loaded, loaded_part, stored = take(7)
     go_send, go_recv, back_send, back_recv = take(4)
 
     me = lax.axis_index("ctx")
@@ -89,14 +89,18 @@
             for place, (there, here) in enumerate(((key, key_here), (value, value_here)))
         ]
 
+    def gated_store(part):
+        at = pl.ds(part * span, span)
+        return pltpu.make_async_copy(gated.at[:, at], gated_out.at[:, at], stored.at[part])
+
     whole_copies = [
         pltpu.make_async_copy(there, here, loaded.at[place])
         for place, (there, here) in enumerate(
-            ((taps, taps_here), (pairs, pairs_here), (bias, bias_here), (query, query_here), (gain, gain_here))
+            ((taps, taps_here), (pairs, pairs_here), (bias, bias_here), (query, query_here))
         )
     ]
-    taps_load, pairs_load, bias_load, query_load, gain_load = whole_copies
-    table_load = pltpu.make_async_copy(table, table_here, loaded.at[5])
+    taps_load, pairs_load, bias_load, query_load = whole_copies
+    table_load = pltpu.make_async_copy(table, table_here, loaded.at[4])
 
     strip = taps_flipped.shape[0] // plan.workers
 
@@ -180,7 +184,7 @@
     for part in parts:
         for copy in column_copies(part):
             copy.start()
-    for copy in (pairs_load, bias_load, query_load, gain_load):
+    for copy in (pairs_load, bias_load, query_load):
         copy.start()
 
     taps_load.wait()
@@ -330,6 +334,7 @@
             product = query_here[:, at].astype(F32) * (conv + bias_here[:, at] * signal)
             gated[:, at] = product
             sums = sums + product * product
+        gated_store(part).start()
 
     squares[half] = jnp.broadcast_to(jnp.sum(sums, axis=1, keepdims=True), (rows, LANES))
     for step in range(1, plan.halves):
@@ -355,15 +360,39 @@
     whole = squares[0]
     for other in range(1, plan.halves):
         whole = whole + squares[other]
-    scaling = lax.rsqrt(whole / (plan.channels * plan.halves) + 1e-05)
-    gain_load.wait()
-
-    for tile in range(plan.channels // LANES):
-        at = pl.ds(tile * LANES, LANES)
-        out[:, at] = (gated[:, at] * scaling * gain_here[:, at]).astype(BF16)
-
+    scale[...] = lax.rsqrt(whole / (plan.channels * plan.halves) + 1e-05)
+    for part in parts:
+        gated_store(part).wait()
     for step in range(1, plan.halves):
         square_copy(lax.rem(half + step, plan.halves), half).wait_send()
+
+
+def rescale(pieces, gated, scale, gain, out, *scratch):
+    gated_here, scale_here, gain_here, out_here, small, loaded, stored = scratch
+    width = gated.shape[1] // pieces
+    columns = [pl.ds(piece * width, width) for piece in range(pieces)]
+    loads = [
+        pltpu.make_async_copy(gated.at[:, at], gated_here.at[:, at], loaded.at[piece])
+        for piece, at in enumerate(columns)
+    ]
+    stores = [
+        pltpu.make_async_copy(out_here.at[:, at], out.at[:, at], stored.at[piece])
+        for piece, at in enumerate(columns)
+    ]
+    scale_load = pltpu.make_async_copy(scale, scale_here, small.at[0])
+    gain_load = pltpu.make_async_copy(gain, gain_here, small.at[1])
+    for copy in [scale_load, gain_load] + loads:
+        copy.start()
+    scale_load.wait()
+    gain_load.wait()
+    for piece in range(pieces):
+        loads[piece].wait()
+        for first in range(piece * width, (piece + 1) * width, LANES):
+            at = pl.ds(first, LANES)
+            out_here[:, at] = (gated_here[:, at] * scale_here[...] * gain_here[:, at]).astype(BF16)
+        stores[piece].start()
+    for store in stores:
+        store.wait()
 
 
 def body(mesh, query, key, value, filter_taps, conv_bias, norm_gain, pair_list):
@@ -384,7 +413,6 @@
         pltpu.VMEM((rows, channels), BF16),
         pltpu.VMEM(filter_taps.shape, F32),
         pltpu.VMEM((1, channels), F32),
-        pltpu.VMEM((1, channels), F32),
         pltpu.VMEM((rows, channels), F32),
         pltpu.VMEM((channels, LANES), BF16),
         pltpu.VMEM((plan.filters, LANES), F32),
@@ -400,14 +428,17 @@
     scratch += [pltpu.VMEM(part_piece, BF16)] * parts
     scratch += [pltpu.VMEM(part_piece, BF16)] * parts
     scratch += [sems((1,)), sems((1,)), sems((plan.halves,)), sems((plan.halves,))]
-    scratch += [sems((6,)), sems((parts, 2))]
+    scratch += [sems((5,)), sems((parts, 2)), sems((parts,))]
     scratch += [sems((parts,))] * 4
     pairs = blocks * (blocks + 2) // 4
-    return pl.pallas_call(
+    gated, scale = pl.pallas_call(
         functools.partial(kernel, plan),
-        out_shape=jax.ShapeDtypeStruct((rows, channels), BF16),
-        in_specs=[hbm] * 7,
-        out_specs=vmem,
+        out_shape=(
+            jax.ShapeDtypeStruct((rows, channels), F32),
+            jax.ShapeDtypeStruct((rows, LANES), F32),
+        ),
+        in_specs=[hbm] * 6,
+        out_specs=(hbm, vmem),
         scratch_shapes=scratch,
         compiler_params=pltpu.CompilerParams(
             collective_id=0, has_side_effects=True, vmem_limit_bytes=VMEM_BYTES
@@ -417,7 +448,27 @@
             bytes_accessed=8 * rows * channels,
             transcendentals=0,
         ),
-    )(pair_list.T, query, key, value, filter_taps, conv_bias[None, :], norm_gain[None, :])
+    )(pair_list.T, query, key, value, filter_taps, conv_bias[None, :])
+    pieces = 4
+    return pl.pallas_call(
+        functools.partial(rescale, pieces),
+        out_shape=jax.ShapeDtypeStruct((rows, channels), BF16),
+        in_specs=[hbm] * 3,
+        out_specs=hbm,
+        scratch_shapes=[
+            pltpu.VMEM((rows, channels), F32),
+            pltpu.VMEM((rows, LANES), F32),
+            pltpu.VMEM((1, channels), F32),
+            pltpu.VMEM((rows, channels), BF16),
+            sems((2,)),
+            sems((pieces,)),
+            sems((pieces,)),
+        ],
+        compiler_params=pltpu.CompilerParams(vmem_limit_bytes=VMEM_BYTES),
+        cost_estimate=pl.CostEstimate(
+            flops=2 * rows * channels, bytes_accessed=6 * rows * channels, transcendentals=0
+        ),
+    )(gated, scale, norm_gain[None, :])
 
 
 def solution(mesh):

time: 37.3 us -> 36 us (0.965)
  local copies, waits for them, and re-layouts: 3.71 us -> 0 us
  Pallas kernels: 33.2 us -> 35.9 us
    unnamed x9 -> x0, local copies, waits for them, and re-layouts: 3.71 us -> none
    pallas_call x1 -> x2, Pallas kernels: 33.2 us -> 35.9 us  [the longest x1 33.9 us: body(): pl.pallas_call(functools.partial(kernel, plan), out_shape=(jax.ShapeDtype...]
where the time goes in v1:
time: 36 us; the launch traced here: 35.9 us
  Pallas kernels  35.9 us (100%)
    pallas_call x1, Pallas kernels, body(): pl.pallas_call(functools.partial(kernel, plan), out_shape=(jax.ShapeDtype...  33.9 us
    pallas_call x1, Pallas kernels, body(): pl.pallas_call(functools.partial(rescale, pieces), out_shape=jax.ShapeDty...  2.01 us

profile of v1, /device:TPU:0, one launch (start us, length us, event | category | flops | bytes accessed | tf_op | source)
XLA Modules:
  0.0 35.9 jit_solution(10227499792537326659)
XLA Ops:
  0.0 33.9 %shard_map.73 = (f32[128,2048]{1,0:T(8,128)}, f32[128,128]{1,0:T(8,128)}) custom-call(s32[3,136]{1,0:T(4,128)} %bitcast.5, bf16[128,2048]{1,0:T(8,128)(2,1)} %query.1, bf16[128,2048]{1,0:T(8,128)(2,1)} %key.1, bf16[128,2048]{1,0:T(8,128)(2,1)} %value.1, f32[128,128]{1,0:T(8,128)} %taps.1, f32[1,2048]{1,0:T(1,128)} %bitcast.4), custom_call_target="tpu_custom_call" | custom-call | flops 603979776 | bytes 2097152 | tf_op jit(solution)/shard_map/pallas_call | solution.py:434
  33.9 2.0 %shard_map.74 = bf16[128,2048]{1,0:T(8,128)(2,1)} custom-call(f32[128,2048]{1,0:T(8,128)} %get-tuple-element.7.gated, f32[128,128]{1,0:T(8,128)} %get-tuple-element.8.scale, f32[1,2048]{1,0:T(1,128)} %bitcast.3), custom_call_target="tpu_custom_call" | custom-call | flops 524288 | bytes 1572864 | tf_op jit(solution)/shard_map/pallas_call | solution.py:453

commit v2 on v1

--- a/solution.py
+++ b/solution.py
@@ -26,7 +26,7 @@
         self.each = max(1, filters // self.blocks)
         self.workers = filters // self.each
         self.share = self.each * self.group
-        self.parts = 4 if self.each % 4 == 0 else 1
+        self.parts = 2 if self.each % 2 == 0 else 1
         self.each_part = self.each // self.parts
         self.share_part = self.share // self.parts
         self.span = channels // self.parts

time: 36 us -> 36 us (level)
  no operation moved by 1% of the time
where the time goes in v2:
time: 36 us; the launch traced here: 35.9 us
  Pallas kernels  35.9 us (100%)
    pallas_call x1, Pallas kernels, body(): pl.pallas_call(functools.partial(kernel, plan), out_shape=(jax.ShapeDtype...  33.9 us
    pallas_call x1, Pallas kernels, body(): pl.pallas_call(functools.partial(rescale, pieces), out_shape=jax.ShapeDty...  2.01 us

profile of v2, /device:TPU:0, one launch (start us, length us, event | category | flops | bytes accessed | tf_op | source)
XLA Modules:
  0.0 35.9 jit_solution(5607756111237580909)
XLA Ops:
  0.0 33.9 %shard_map.73 = (f32[128,2048]{1,0:T(8,128)}, f32[128,128]{1,0:T(8,128)}) custom-call(s32[3,136]{1,0:T(4,128)} %bitcast.5, bf16[128,2048]{1,0:T(8,128)(2,1)} %query.1, bf16[128,2048]{1,0:T(8,128)(2,1)} %key.1, bf16[128,2048]{1,0:T(8,128)(2,1)} %value.1, f32[128,128]{1,0:T(8,128)} %taps.1, f32[1,2048]{1,0:T(1,128)} %bitcast.4), custom_call_target="tpu_custom_call" | custom-call | flops 603979776 | bytes 2097152 | tf_op jit(solution)/shard_map/pallas_call | solution.py:434
  33.9 2.0 %shard_map.74 = bf16[128,2048]{1,0:T(8,128)(2,1)} custom-call(f32[128,2048]{1,0:T(8,128)} %get-tuple-element.7.gated, f32[128,128]{1,0:T(8,128)} %get-tuple-element.8.scale, f32[1,2048]{1,0:T(1,128)} %bitcast.3), custom_call_target="tpu_custom_call" | custom-call | flops 524288 | bytes 1572864 | tf_op jit(solution)/shard_map/pallas_call | solution.py:453

commit v3 on v2

--- a/solution.py
+++ b/solution.py
@@ -266,16 +266,14 @@
             got[part][me] = flipped[pl.ds(first, part_rows), :]
 
         arrived(taps_got.at[pl.ds(0, (blocks - 1) * strip)], taps_recv.at[0])
-        spread_taps(0)
+        for part in parts:
+            spread_taps(part)
 
     table_load.wait()
 
     @only_worker(me)
     def _():
         for part in parts:
-            if part > 0:
-                spread_taps(part)
-
             arrived(got[part].at[pl.ds(0, blocks - 1)], go_recv.at[part])
 
             def in_order(block, part=part):

time: 36 us -> 36 us (level)
  no operation moved by 1% of the time
where the time goes in v3:
time: 36 us; the launch traced here: 35.9 us
  Pallas kernels  35.9 us (100%)
    pallas_call x1, Pallas kernels, body(): pl.pallas_call(functools.partial(kernel, plan), out_shape=(jax.ShapeDtype...  33.9 us
    pallas_call x1, Pallas kernels, body(): pl.pallas_call(functools.partial(rescale, pieces), out_shape=jax.ShapeDty...  2.01 us

profile of v3, /device:TPU:0, one launch (start us, length us, event | category | flops | bytes accessed | tf_op | source)
XLA Modules:
  0.0 35.9 jit_solution(509980254534633322)
XLA Ops:
  0.0 33.9 %shard_map.73 = (f32[128,2048]{1,0:T(8,128)}, f32[128,128]{1,0:T(8,128)}) custom-call(s32[3,136]{1,0:T(4,128)} %bitcast.5, bf16[128,2048]{1,0:T(8,128)(2,1)} %query.1, bf16[128,2048]{1,0:T(8,128)(2,1)} %key.1, bf16[128,2048]{1,0:T(8,128)(2,1)} %value.1, f32[128,128]{1,0:T(8,128)} %taps.1, f32[1,2048]{1,0:T(1,128)} %bitcast.4), custom_call_target="tpu_custom_call" | custom-call | flops 603979776 | bytes 2097152 | tf_op jit(solution)/shard_map/pallas_call | solution.py:432
  33.9 2.0 %shard_map.74 = bf16[128,2048]{1,0:T(8,128)(2,1)} custom-call(f32[128,2048]{1,0:T(8,128)} %get-tuple-element.7.gated, f32[128,128]{1,0:T(8,128)} %get-tuple-element.8.scale, f32[1,2048]{1,0:T(1,128)} %bitcast.3), custom_call_target="tpu_custom_call" | custom-call | flops 524288 | bytes 1572864 | tf_op jit(solution)/shard_map/pallas_call | solution.py:451

commit v4 on v3

--- a/solution.py
+++ b/solution.py
@@ -89,9 +89,9 @@
             for place, (there, here) in enumerate(((key, key_here), (value, value_here)))
         ]
 
-    def gated_store(part):
-        at = pl.ds(part * span, span)
-        return pltpu.make_async_copy(gated.at[:, at], gated_out.at[:, at], stored.at[part])
+    def gated_store(piece):
+        at = pl.ds(piece * (span // 4), span // 4)
+        return pltpu.make_async_copy(gated.at[:, at], gated_out.at[:, at], stored.at[piece])
 
     whole_copies = [
         pltpu.make_async_copy(there, here, loaded.at[place])
@@ -332,7 +332,8 @@
             product = query_here[:, at].astype(F32) * (conv + bias_here[:, at] * signal)
             gated[:, at] = product
             sums = sums + product * product
-        gated_store(part).start()
+            if (tile + 1) % (part_tiles // 4) == 0:
+                gated_store(tile // (part_tiles // 4)).start()
 
     squares[half] = jnp.broadcast_to(jnp.sum(sums, axis=1, keepdims=True), (rows, LANES))
     for step in range(1, plan.halves):
@@ -359,8 +360,8 @@
     for other in range(1, plan.halves):
         whole = whole + squares[other]
     scale[...] = lax.rsqrt(whole / (plan.channels * plan.halves) + 1e-05)
-    for part in parts:
-        gated_store(part).wait()
+    for piece in range(4 * plan.parts):
+        gated_store(piece).wait()
     for step in range(1, plan.halves):
         square_copy(lax.rem(half + step, plan.halves), half).wait_send()
 
@@ -426,7 +427,7 @@
     scratch += [pltpu.VMEM(part_piece, BF16)] * parts
     scratch += [pltpu.VMEM(part_piece, BF16)] * parts
     scratch += [sems((1,)), sems((1,)), sems((plan.halves,)), sems((plan.halves,))]
-    scratch += [sems((5,)), sems((parts, 2)), sems((parts,))]
+    scratch += [sems((5,)), sems((parts, 2)), sems((4 * parts,))]
     scratch += [sems((parts,))] * 4
     pairs = blocks * (blocks + 2) // 4
     gated, scale = pl.pallas_call(

time: 36 us -> 36.1 us (level)
  no operation moved by 1% of the time
where the time goes in v4:
time: 36.1 us; the launch traced here: 35.9 us
  Pallas kernels  35.9 us (99%)
    pallas_call x1, Pallas kernels, body(): pl.pallas_call(functools.partial(kernel, plan), out_shape=(jax.ShapeDtype...  33.9 us
    pallas_call x1, Pallas kernels, body(): pl.pallas_call(functools.partial(rescale, pieces), out_shape=jax.ShapeDty...  2.01 us

profile of v4, /device:TPU:0, one launch (start us, length us, event | category | flops | bytes accessed | tf_op | source)
XLA Modules:
  0.0 35.9 jit_solution(18336293744404341117)
XLA Ops:
  0.0 33.9 %shard_map.73 = (f32[128,2048]{1,0:T(8,128)}, f32[128,128]{1,0:T(8,128)}) custom-call(s32[3,136]{1,0:T(4,128)} %bitcast.5, bf16[128,2048]{1,0:T(8,128)(2,1)} %query.1, bf16[128,2048]{1,0:T(8,128)(2,1)} %key.1, bf16[128,2048]{1,0:T(8,128)(2,1)} %value.1, f32[128,128]{1,0:T(8,128)} %taps.1, f32[1,2048]{1,0:T(1,128)} %bitcast.4), custom_call_target="tpu_custom_call" | custom-call | flops 603979776 | bytes 2097152 | tf_op jit(solution)/shard_map/pallas_call | solution.py:433
  33.9 2.0 %shard_map.74 = bf16[128,2048]{1,0:T(8,128)(2,1)} custom-call(f32[128,2048]{1,0:T(8,128)} %get-tuple-element.7.gated, f32[128,128]{1,0:T(8,128)} %get-tuple-element.8.scale, f32[1,2048]{1,0:T(1,128)} %bitcast.3), custom_call_target="tpu_custom_call" | custom-call | flops 524288 | bytes 1572864 | tf_op jit(solution)/shard_map/pallas_call | solution.py:452
